TPU v7x, 256 devices: a whole 4x4x8 slice. The times are simulated.
256 devices in a mesh: expert: 32 (over x_lo, z, core), dp: 8 (over x_hi, y).
Axes of the slice: x: 4 (x_hi: 2, x_lo: 2; x = x_hi * 2 + x_lo), y: 4, z: 8, core: 2. Of those that a mesh axis runs over, the one named last changes fastest.
Arguments:
- tokens: bfloat16 [16384, 2048], P(('expert', 'dp')), may hold values from -6 to 6
- expert_ids: int32 [16384, 2], P(('expert', 'dp')), may hold values from 0 to 31, as said below
- gate_codes: int32 [16384, 2], P(('expert', 'dp')), may hold values from 1 to 4095
- expert_order: int32 [32], replicated, may hold values from 0 to 31, each once
- w_gate: bfloat16 [32, 2048, 7168], P('expert', None, 'dp'), may hold values from -0.125 to 0.125
- w_up: bfloat16 [32, 2048, 7168], P('expert', None, 'dp'), may hold values from -0.125 to 0.125
- w_down: bfloat16 [32, 7168, 2048], P('expert', 'dp'), may hold values from -0.0625 to 0.0625
Outputs:
- mixed: bfloat16 [16384, 2048], P(('expert', 'dp'))
Inputs may be any that keep to these rules, and one draw needn't show every extreme that they name: `expert_ids`: in each aligned block of 64 tokens (the tokens of one device), every id below 2 is named by exactly 8 tokens, and every other id by at most 4 tokens, some of them by exactly 4. A token's two ids differ. `expert_order`: each expert number appears once.
All inputs are finite; a program needn't handle non-finite values.
Results may differ from a plain program's by a relative error of at most 0.017.
Values may be sent and summed in bfloat16 or wider, within the bound.
No kernel may reach another device: no remote copies, remote signals or barrier semaphores. Data moves between devices by JAX's collectives and lax.ppermute only.
A program may use at most 128 MiB of HBM per device.

v0:
```python
import jax
import jax.numpy as jnp
from jax import lax
from jax.sharding import PartitionSpec as P

HOT = 2


def spread(block, axis, owner):
    block = jnp.where(lax.axis_index(axis) == owner, block, jnp.zeros_like(block))
    return lax.psum(block, axis)


def expert_block(token_rows, gate_slice, up_slice, down_slice):
    gathered = lax.all_gather(token_rows, "dp", axis=0, tiled=True)
    gate_value = jnp.dot(gathered, gate_slice, preferred_element_type=jnp.float32)
    up_value = jnp.dot(gathered, up_slice, preferred_element_type=jnp.float32)
    hidden = (jax.nn.silu(gate_value) * up_value).astype(jnp.bfloat16)
    return lax.psum_scatter(
        jnp.dot(hidden, down_slice, preferred_element_type=jnp.float32).astype(jnp.bfloat16),
        "dp",
        scatter_dimension=0,
        tiled=True,
    ).astype(jnp.float32)


def place_rows(member, slot_count, repeated):
    member_int = member.astype(jnp.int32)
    before = jnp.cumsum(member_int, axis=0) - member_int
    slot_rank = jnp.sum(before * member_int, axis=1)
    column_ids = jnp.arange(member.shape[1], dtype=jnp.int32)
    column = jnp.sum(member_int * column_ids[None, :], axis=1)
    is_valid = jnp.any(member, axis=1)
    slot_index = jnp.where(is_valid, column * slot_count + slot_rank, -1)
    slot_ids = jnp.arange(member.shape[1] * slot_count, dtype=jnp.int32)
    pick_table = (slot_index[None, :] == slot_ids[:, None]).astype(jnp.bfloat16)
    filled = jnp.dot(pick_table, repeated, preferred_element_type=jnp.float32).astype(jnp.bfloat16)
    return (slot_index, filled)


def per_device(tokens, expert_ids, gate_codes, expert_order, w_gate, w_up, w_down):
    n_experts = lax.axis_size("expert")
    local_tokens = tokens.shape[0]
    width = tokens.shape[1]
    hot_rows = local_tokens // 8
    cold_slots = 2 * local_tokens - HOT * hot_rows
    cold_most = -(-cold_slots // (n_experts - HOT))
    gate_slice = w_gate[0]
    up_slice = w_up[0]
    down_slice = w_down[0]
    gate_real = gate_codes.astype(jnp.float32)
    weights = gate_real / jnp.sum(gate_real, axis=1, keepdims=True)
    chosen = expert_ids.reshape(-1)
    expert_range = jnp.arange(n_experts, dtype=jnp.int32)
    id_match = chosen[:, None] == expert_range[None, :]
    physical = jnp.sum(jnp.where(id_match, expert_order[None, :], 0), axis=1)
    repeated = jnp.repeat(tokens, 2, axis=0)
    is_hot = chosen < HOT
    eligible = jnp.logical_not(is_hot)
    member = jnp.logical_and(physical[:, None] == expert_range[None, :], eligible[:, None])
    slot_index, send_rows = place_rows(member, cold_most, repeated)
    send_rows = send_rows.reshape(n_experts, cold_most, width)
    received = lax.all_to_all(send_rows, "expert", split_axis=0, concat_axis=0, tiled=True)
    sources = received.shape[0]
    slots_here = received.shape[1]
    flat_rows = received.reshape(sources * slots_here, width)
    summed = expert_block(flat_rows, gate_slice, up_slice, down_slice)
    rounded = summed.astype(jnp.bfloat16).reshape(sources, slots_here, width)
    returned_rows = lax.all_to_all(rounded, "expert", split_axis=0, concat_axis=0, tiled=True)
    returned_flat = returned_rows.reshape(n_experts * cold_most, width)
    routed_part = returned_flat[jnp.maximum(slot_index, 0)]
    hot_range = jnp.arange(HOT, dtype=jnp.int32)
    hot_member = chosen[:, None] == hot_range[None, :]
    hot_slot, hot_send = place_rows(hot_member, hot_rows, repeated)
    results = []
    for position in range(HOT):
        owner_index = expert_order[position]
        shadow_gate, shadow_up, shadow_down = (
            spread(gate_slice, "expert", owner_index),
            spread(up_slice, "expert", owner_index),
            spread(down_slice, "expert", owner_index),
        )
        rows_here = hot_send[position * hot_rows : (position + 1) * hot_rows]
        results.append(
            expert_block(rows_here, shadow_gate, shadow_up, shadow_down).astype(jnp.bfloat16)
        )
    hot_out = jnp.concatenate(results, axis=0)
    hot_part = hot_out[jnp.maximum(hot_slot, 0)]
    picked = jnp.where(is_hot[:, None], hot_part, routed_part)
    picked_real = picked.reshape(local_tokens, 2, width).astype(jnp.float32)
    mixed = jnp.sum(weights[:, :, None] * picked_real, axis=1)
    return mixed.astype(jnp.bfloat16)


def solution(mesh):
    in_specs = (
        P(("expert", "dp"), None),
        P(("expert", "dp"), None),
        P(("expert", "dp"), None),
        P(),
        P("expert", None, "dp"),
        P("expert", None, "dp"),
        P("expert", "dp", None),
    )
    out_specs = P(("expert", "dp"), None)
    return jax.shard_map(
        per_device, mesh=mesh, in_specs=in_specs, out_specs=out_specs, check_vma=False
    )
```

profile of v0, /device:TPU:8, one launch (start us, length us, event | category | flops | bytes accessed | tf_op | source)
XLA Modules:
  0.0 617.8 jit_solution(16100432951603813389)
XLA Ops:
  7.4 0.8 copy.13
  8.1 0.1 eq.40
  8.3 1.3 broadcast_in_dim.26
  9.5 0.2 reshape.117
  9.8 0.8 select_reduce_fusion.2
  10.6 0.2 fusion.24
  10.8 0.2 reduce_window_sum.23
  11.0 0.2 select_reduce_fusion.1
  11.2 0.3 convolution_convert_fusion.1
  11.5 0.2 reshape.118
  11.7 28.0 %all_to_all.10 = bf16[32,4,2048]{2,1,0:T(4,128)(2,1)S(1)} all-to-all(bf16[32,4,2048]{2,1,0:T(4,128)(2,1)S(1)} %reshape.118), channel_id=1, replica_groups=mesh['expert'=32,'dp'=8] {'expert'}, dimensions={0} | all-to-all | bytes 1048576 | tf_op jit(solution)/shard_map/all_to_all | solution.py:63
  39.7 0.9 reshape.119
  40.7 71.8 %all-gather.2.cloned.1.call-done = bf16[1024,2048]{1,0:T(8,128)(2,1)} async-done(((bf16[128,2048]{1,0:T(8,128)(2,1)}), bf16[1024,2048]{1,0:T(8,128)(2,1)}) %all-gather.2.cloned.1.call-update) | async-done | bytes 4194320 | tf_op jit(solution)/shard_map/all_gather | solution.py:15
  112.5 7.5 %fusion.1 = f32[1024,896]{1,0:T(8,128)S(1)} fusion(bf16[1024,2048]{1,0:T(8,128)(2,1)} %all-gather.2.cloned.1.call-done, bf16[1,2048,896]{2,1,0:T(8,128)(2,1)} %param.12), kind=kOutput, calls=%fused_computation.6 | convolution fusion | flops 3758096384 | bytes 11534336 | tf_op jit(solution)/shard_map/dot_general | solution.py:17
  120.0 4.8 multiply_convert_fusion
  124.8 6.1 convolution_convert_fusion
  130.9 0.0 all-reduce.3.cloned.1.call-start
  131.0 0.6 copy-done.4
  131.6 0.6 fusion.31
  133.4 5.8 bitcast_select_fusion.1
  139.2 5.5 bitcast_select_fusion.3
  144.7 0.2 fusion.21
  144.9 0.2 reduce_window_sum.22
  145.1 0.3 copy-done.6
  145.4 0.2 select_reduce_fusion.4
  145.6 0.2 convolution_convert_fusion.4
  145.8 53.7 %all_gather.9 = bf16[64,2048]{1,0:T(8,128)(2,1)S(1)} all-gather(bf16[8,2048]{1,0:T(8,128)(2,1)S(1)} %get-tuple-element.25), channel_id=1, replica_groups=mesh['expert'=32,'dp'=8] {'dp'}, dimensions={0}, use_global_device_ids=true | all-gather | bytes 294912 | tf_op jit(solution)/shard_map/all_gather | solution.py:15
  199.4 60.8 %all_gather.10 = bf16[64,2048]{1,0:T(8,128)(2,1)S(1)} all-gather(bf16[8,2048]{1,0:T(8,128)(2,1)S(1)} %get-tuple-element.26), channel_id=1, replica_groups=mesh['expert'=32,'dp'=8] {'dp'}, dimensions={0}, use_global_device_ids=true | all-gather | bytes 294912 | tf_op jit(solution)/shard_map/all_gather | solution.py:15
  260.2 52.5 %reduce-scatter.8.cloned.1.call-done = bf16[128,2048]{1,0:T(8,128)(2,1)} async-done(((bf16[1024,2048]{1,0:T(8,128)(2,1)}), bf16[128,2048]{1,0:T(8,128)(2,1)}) %reduce-scatter.8.cloned.1.call-update) | async-done | bytes 524304 | tf_op jit(solution)/shard_map/reduce_scatter | solution.py:19
  312.7 2.0 reshape.120
  314.8 5.9 all-to-all-start.1
  320.7 0.2 reduce-scatter.4.cloned.1.call-start
  320.9 126.6 %all-reduce.3.cloned.1.call-done = (bf16[896,2048]{1,0:T(8,128)(2,1)}, bf16[2048,896]{1,0:T(8,128)(2,1)}, bf16[2048,896]{1,0:T(8,128)(2,1)}, bf16[896,2048]{1,0:...) async-done(((bf16[896,2048]{1,0:T(8,128)(2,1)}, bf16[2048,896]{1,0:T(8,128)(2,1)}, bf16[2048,896]{1,0:T(8,128)(2,1)}, bf16[896,2048]{1,0:T(8,128)(2,1)}, ...) | async-done | bytes 22020112 | tf_op jit(solution)/shard_map/psum | solution.py:11
  447.5 2.7 fusion.32
  450.3 5.4 convolution_convert_fusion.3
  455.8 2.7 fusion.33
  458.5 5.4 convolution_convert_fusion.2
  464.0 0.1 copy.11
  464.1 0.1 copy.12
  464.2 0.1 reshape.121
  464.3 0.9 gather_fusion.1
  465.3 0.3 gather.13
  465.6 61.9 %reduce-scatter.4.cloned.1.call-done = bf16[8,2048]{1,0:T(8,128)(2,1)} async-done(((bf16[64,2048]{1,0:T(8,128)(2,1)}), bf16[8,2048]{1,0:T(8,128)(2,1)}) %reduce-scatter.4.cloned.1.call-update) | async-done | bytes 32784 | tf_op jit(solution)/shard_map/reduce_scatter | solution.py:19
  527.5 78.0 %reduce-scatter.6.cloned.1.call-done = bf16[8,2048]{1,0:T(8,128)(2,1)} async-done(((bf16[64,2048]{1,0:T(8,128)(2,1)}), bf16[8,2048]{1,0:T(8,128)(2,1)}) %reduce-scatter.6.cloned.1.call-update) | async-done | bytes 32784 | tf_op jit(solution)/shard_map/reduce_scatter | solution.py:19
  605.6 0.8 pad_maximum_fusion
  606.3 0.9 gather_fusion
  607.3 0.3 gather.11
  607.6 3.0 multiply_reduce_fusion
  (32 shorter events, 0.3 us)
Async XLA Ops:
  7.4 105.1 %all-gather.2.cloned.1.call-start = ((), (), s32[]{:S(2)}) async-start(), calls=%async_computation.7 | async-start | bytes 4718592 | tf_op jit(solution)/shard_map/all_gather | solution.py:15
  40.6 272.1 %reduce-scatter.8.cloned.1.call-start = ((), (), s32[]{:S(2)}) async-start(), calls=%async_computation.8 | async-start | bytes 4718592 | tf_op jit(solution)/shard_map/reduce_scatter | solution.py:19
  112.5 7.5 %copy-start.2 = (bf16[1,2048,896]{2,1,0:T(8,128)(2,1)S(1)}, bf16[1,2048,896]{2,1,0:T(8,128)(2,1)}, u32[]{:S(2)}) copy-start(bf16[1,2048,896]{2,1,0:T(8,128)(2,1)} %param.11) | copy-start | bytes 11010052
  112.5 7.5 %copy-start.7 = (bf16[1024,2048]{1,0:T(8,128)(2,1)S(1)}, bf16[1024,2048]{1,0:T(8,128)(2,1)}, u32[]{:S(2)}) copy-start(bf16[1024,2048]{1,0:T(8,128)(2,1)} %all-gather.2.cloned.1.call-done) | copy-start | bytes 12582916
  120.0 4.8 copy-start
  130.9 0.7 copy-start.4
  130.9 316.6 %all-reduce.3.cloned.1.call-start = ((), (), s32[]{:S(2)}) async-start(), calls=%async_computation.9 | async-start | bytes 44040192 | tf_op jit(solution)/shard_map/psum | solution.py:11
  133.4 5.8 copy-start.1
  133.4 5.8 copy-start.3
  144.7 0.7 copy-start.6
  314.8 149.5 %all-to-all-start.1 = ((bf16[32,4,2048]{2,1,0:T(4,128)(2,1)}), bf16[32,4,2048]{2,1,0:T(4,128)(2,1)S(1)}, u32[]{:S(2)}, u32[]{:S(2)}) async-start(bf16[32,4,2048]{2,1,0:T(4,128)(2,1)} %reshape.120), calls=%async_computation.4 | async-start | bytes 1048576 | tf_op jit(solution)/shard_map/all_to_all | solution.py:69
  320.7 206.9 %reduce-scatter.4.cloned.1.call-start = ((), (), s32[]{:S(2)}) async-start(), calls=%async_computation.5 | async-start | bytes 294912 | tf_op jit(solution)/shard_map/reduce_scatter | solution.py:19
  455.7 149.9 %reduce-scatter.6.cloned.1.call-start = ((), (), s32[]{:S(2)}) async-start(), calls=%async_computation.6 | async-start | bytes 294912 | tf_op jit(solution)/shard_map/reduce_scatter | solution.py:19
  458.5 5.6 copy-start.5
Sparse Core Ops, SparseCore 0:
  40.8 71.6 all-gather.1
  131.0 181.6 reduce-scatter.7
  455.8 71.6 reduce-scatter.3
  531.7 73.8 reduce-scatter.5
Sparse Core Ops, SparseCore 1:
  144.8 302.7 all-reduce.2
where the time goes:
time: 618 us
  waiting for transfers between devices  391 us (63%)
  blocking collectives  142 us (23%)
  matrix products  35.1 us (6%)
  other arithmetic  17 us (3%)
  between operations  16.1 us (3%)
  local copies, waits for them, and re-layouts  9.88 us (2%)
  starting transfers between devices  6.24 us (1%)
    reduce_scatter x3, waiting for transfers between devices, expert_block(): lax.psum_scatter(jnp.dot(hidden, down_slice, preferred_element_type=jnp.f...  192 us
    psum x1, waiting for transfers between devices, spread(): return lax.psum(block, axis)  127 us
    all_gather x2, blocking collectives, expert_block(): gathered = lax.all_gather(token_rows, 'dp', axis=0, tiled=True)  114 us
    all_gather x1, waiting for transfers between devices, expert_block(): gathered = lax.all_gather(token_rows, 'dp', axis=0, tiled=True)  71.8 us
    all_to_all x1, blocking collectives, per_device(): lax.all_to_all(send_rows, 'expert', split_axis=0, concat_axis=0, tiled=True)  28 us
    dot_general x3, matrix products, expert_block(): jnp.dot(hidden, down_slice, preferred_element_type=jnp.float32)  16.9 us
  transfers between devices with their start and end apart: 6, of which 5 were waited for; matrix products, arithmetic and copies ran while one was open for 5% of the time, Pallas kernels for 0%

commit v1 on v0

--- a/solution.py
+++ b/solution.py
@@ -12,7 +12,9 @@
 
 
 def expert_block(token_rows, gate_slice, up_slice, down_slice):
-    gathered = lax.all_gather(token_rows, "dp", axis=0, tiled=True)
+    gathered = jnp.concatenate(
+        lax.all_to_all(jnp.stack([token_rows] * lax.axis_size("dp")), "dp", 0, 0), axis=0
+    )
     gate_value = jnp.dot(gathered, gate_slice, preferred_element_type=jnp.float32)
     up_value = jnp.dot(gathered, up_slice, preferred_element_type=jnp.float32)
     hidden = (jax.nn.silu(gate_value) * up_value).astype(jnp.bfloat16)

time: 618 us -> 584 us (0.945)
  blocking collectives: 142 us -> 82.8 us
  waiting for transfers between devices: 391 us -> 410 us
  starting transfers between devices: 6.24 us -> 15.2 us
    all_gather x2 -> x0, blocking collectives: 114 us -> none  [expert_block(): gathered = lax.all_gather(token_rows, 'dp', axis=0, tiled=True)]
    reduce_scatter x3, waiting for transfers between devices: 192 us -> 281 us  [expert_block(): lax.psum_scatter(jnp.dot(hidden, down_slice, preferred_element_type=jnp.f...]
    all_gather x1 -> x0, waiting for transfers between devices: 71.8 us -> none  [expert_block(): gathered = lax.all_gather(token_rows, 'dp', axis=0, tiled=True)]
    all_to_all x0 -> x1, blocking collectives: none -> 54.7 us  [expert_block(): lax.all_to_all(jnp.stack([token_rows] * lax.axis_size('dp')), 'dp', 0, 0)]
    all_to_all x0 -> x2, starting transfers between devices: none -> 10.9 us  [expert_block(): lax.all_to_all(jnp.stack([token_rows] * lax.axis_size('dp')), 'dp', 0, 0)]
    all_to_all x1, waiting for transfers between devices: 0.01 us -> 10 us  [per_device(): lax.all_to_all(rounded, 'expert', split_axis=0, concat_axis=0, tiled=True)]
    psum x1, waiting for transfers between devices: 127 us -> 118 us  [spread(): return lax.psum(block, axis)]
  transfers between devices with their start and end apart: 6 -> 7, of which waited for: 5 -> 5; matrix products, arithmetic and copies ran while one was open for 5% -> 6% of each run, Pallas kernels for 0% -> 0%
where the time goes in v1:
time: 584 us; the launch traced here: 583 us
  waiting for transfers between devices  410 us (70%)
  blocking collectives  82.8 us (14%)
  matrix products  32.1 us (5%)
  other arithmetic  17 us (3%)
  between operations  16.1 us (3%)
  starting transfers between devices  15.2 us (3%)
  local copies, waits for them, and re-layouts  10.8 us (2%)
    reduce_scatter x3, waiting for transfers between devices, expert_block(): lax.psum_scatter(jnp.dot(hidden, down_slice, preferred_element_type=jnp.f...  281 us
    psum x1, waiting for transfers between devices, spread(): return lax.psum(block, axis)  118 us
    all_to_all x1, blocking collectives, expert_block(): lax.all_to_all(jnp.stack([token_rows] * lax.axis_size('dp')), 'dp', 0, 0)  54.7 us
    all_to_all x1, blocking collectives, per_device(): lax.all_to_all(send_rows, 'expert', split_axis=0, concat_axis=0, tiled=True)  28 us
    dot_general x3, matrix products, expert_block(): jnp.dot(hidden, down_slice, preferred_element_type=jnp.float32)  16.9 us
  transfers between devices with their start and end apart: 7, of which 5 were waited for; matrix products, arithmetic and copies ran while one was open for 6% of the time, Pallas kernels for 0%

profile of v1, /device:TPU:8, one launch (start us, length us, event | category | flops | bytes accessed | tf_op | source)
XLA Modules:
  0.0 583.4 jit_solution(15045623344065865175)
XLA Ops:
  7.4 1.3 broadcast_in_dim.26
  8.6 0.2 reshape.129
  8.8 0.8 copy.13
  9.6 0.1 eq.40
  9.8 0.8 select_reduce_fusion.2
  10.6 0.2 fusion.32
  10.8 0.2 reduce_window_sum.23
  11.0 0.2 select_reduce_fusion.1
  11.2 0.3 convolution_convert_fusion.1
  11.5 0.2 reshape.132
  11.7 28.0 %all_to_all.25 = bf16[32,4,2048]{2,1,0:T(4,128)(2,1)S(1)} all-to-all(bf16[32,4,2048]{2,1,0:T(4,128)(2,1)S(1)} %reshape.132), channel_id=1, replica_groups=mesh['expert'=32,'dp'=8] {'expert'}, dimensions={0} | all-to-all | bytes 1048576 | tf_op jit(solution)/shard_map/all_to_all | solution.py:65
  39.7 0.1 stack_reshape.2
  39.8 0.5 stack.8
  40.4 54.7 %all_to_all.26 = bf16[8,128,2048]{2,1,0:T(8,128)(2,1)S(1)} all-to-all(bf16[8,128,2048]{2,1,0:T(8,128)(2,1)S(1)} %stack.8), channel_id=1, replica_groups=mesh['expert'=32,'dp'=8] {'dp'}, dimensions={0} | all-to-all | bytes 8388608 | tf_op jit(solution)/shard_map/all_to_all | solution.py:16
  95.1 4.5 fusion.1
  99.7 4.8 multiply_convert_fusion
  104.4 6.1 %convolution_convert_fusion = bf16[1024,2048]{1,0:T(8,128)(2,1)} fusion(bf16[1024,896]{1,0:T(8,128)(2,1)S(1)} %multiply_convert_fusion, bf16[1,896,2048]{2,1,0:T(8,128)(2,1)S(1)} %copy-done), kind=kOutput, calls=%fused_computation.2 | convolution fusion | flops 3760193536 | bytes 9699328 | tf_op jit(solution)/shard_map/dot_general | solution.py:22
  110.6 0.6 copy-done.5
  111.1 0.6 fusion.39
  113.0 5.9 %bitcast_select_fusion.1 = (bf16[896,2048]{1,0:T(8,128)(2,1)}, bf16[896,2048]{1,0:T(8,128)(2,1)}) fusion(bf16[1,896,2048]{2,1,0:T(8,128)(2,1)} %param.13, pred[]{:T(512)S(6)} %eq.89, pred[]{:T(512)S(6)} %eq.90), kind=kLoop, calls=%fused_computation.5 | loop fusion | flops 3670016 | bytes 11010050 | tf_op jit(solution)/shard_map/jit(_where)/select_n | solution.py:10
  118.9 5.3 bitcast_select_fusion.3
  124.2 0.2 fusion.29
  124.4 0.2 reduce_window_sum.22
  124.6 0.2 select_reduce_fusion.4
  124.8 0.2 convolution_convert_fusion.4
  125.0 0.7 stack.7
  125.7 5.1 all-to-all-start.1
  130.8 0.1 copy.12
  130.9 154.9 %reduce-scatter.8.cloned.1.call-done = bf16[128,2048]{1,0:T(8,128)(2,1)} async-done(((bf16[1024,2048]{1,0:T(8,128)(2,1)}), bf16[128,2048]{1,0:T(8,128)(2,1)}) %reduce-scatter.8.cloned.1.call-update) | async-done | bytes 524304 | tf_op jit(solution)/shard_map/reduce_scatter | solution.py:21
  285.8 2.1 reshape.134
  287.9 0.7 stack.6
  288.6 5.8 all-to-all-start
  294.4 118.4 %all-reduce.3.cloned.1.call-done = (bf16[896,2048]{1,0:T(8,128)(2,1)}, bf16[2048,896]{1,0:T(8,128)(2,1)}, bf16[2048,896]{1,0:T(8,128)(2,1)}, bf16[896,2048]{1,0:...) async-done(((bf16[896,2048]{1,0:T(8,128)(2,1)}, bf16[2048,896]{1,0:T(8,128)(2,1)}, bf16[2048,896]{1,0:T(8,128)(2,1)}, bf16[896,2048]{1,0:T(8,128)(2,1)}, ...) | async-done | bytes 22020112 | tf_op jit(solution)/shard_map/psum | solution.py:11
  412.8 2.7 fusion.11
  415.6 5.4 convolution_convert_fusion.2
  421.0 4.2 all-to-all-start.4
  425.2 2.7 fusion.15
  428.0 5.4 convolution_convert_fusion.3
  433.6 10.0 %all-to-all-done.4 = bf16[32,4,2048]{2,1,0:T(4,128)(2,1)S(1)} async-done(((bf16[32,4,2048]{2,1,0:T(4,128)(2,1)}), bf16[32,4,2048]{2,1,0:T(4,128)(2,1)S(1)}, u32[]{:S(2)}, u32[]{:S(2)}) %all-to-all-start.4) | async-done | bytes 524320 | tf_op jit(solution)/shard_map/all_to_all | solution.py:71
  443.6 0.1 reshape.135
  443.7 0.9 gather_fusion.1
  444.7 0.3 gather.13
  445.0 48.0 %reduce-scatter.6.cloned.1.call-done = bf16[8,2048]{1,0:T(8,128)(2,1)} async-done(((bf16[64,2048]{1,0:T(8,128)(2,1)}), bf16[8,2048]{1,0:T(8,128)(2,1)}) %reduce-scatter.6.cloned.1.call-update) | async-done | bytes 32784 | tf_op jit(solution)/shard_map/reduce_scatter | solution.py:21
  493.0 78.2 %reduce-scatter.4.cloned.1.call-done = bf16[8,2048]{1,0:T(8,128)(2,1)} async-done(((bf16[64,2048]{1,0:T(8,128)(2,1)}), bf16[8,2048]{1,0:T(8,128)(2,1)}) %reduce-scatter.4.cloned.1.call-update) | async-done | bytes 32784 | tf_op jit(solution)/shard_map/reduce_scatter | solution.py:21
  571.2 0.8 pad_maximum_fusion
  572.0 0.9 gather_fusion
  572.9 0.3 gather.11
  573.3 3.0 multiply_reduce_fusion
  (35 shorter events, 0.4 us)
Async XLA Ops:
  7.4 278.4 %reduce-scatter.8.cloned.1.call-start = ((), (), s32[]{:S(2)}) async-start(), calls=%async_computation.10 | async-start | bytes 4718592 | tf_op jit(solution)/shard_map/reduce_scatter | solution.py:21
  40.4 54.8 %copy-start.1 = (bf16[1,2048,896]{2,1,0:T(8,128)(2,1)S(1)}, bf16[1,2048,896]{2,1,0:T(8,128)(2,1)}, u32[]{:S(2)}) copy-start(bf16[1,2048,896]{2,1,0:T(8,128)(2,1)} %param.12) | copy-start | bytes 11010052
  95.1 4.5 copy-start.3
  99.6 4.8 copy-start
  110.5 0.7 copy-start.5
  110.5 302.3 %all-reduce.3.cloned.1.call-start = ((), (), s32[]{:S(2)}) async-start(), calls=%async_computation.11 | async-start | bytes 44040192 | tf_op jit(solution)/shard_map/psum | solution.py:11
  113.0 5.9 %copy-start.2 = (bf16[1,2048,896]{2,1,0:T(8,128)(2,1)S(1)}, bf16[1,2048,896]{2,1,0:T(8,128)(2,1)}, u32[]{:S(2)}) copy-start(bf16[1,2048,896]{2,1,0:T(8,128)(2,1)} %param.12) | copy-start | bytes 11010052
  113.0 5.9 %copy-start.4 = (bf16[1,2048,896]{2,1,0:T(8,128)(2,1)S(1)}, bf16[1,2048,896]{2,1,0:T(8,128)(2,1)}, u32[]{:S(2)}) copy-start(bf16[1,2048,896]{2,1,0:T(8,128)(2,1)} %param.11) | copy-start | bytes 11010052
  124.2 6.6 %copy-start.6 = (s32[64,2]{0,1:T(2,128)S(1)}, s32[64,2]{0,1:T(2,128)}, u32[]{:S(2)}) copy-start(s32[64,2]{0,1:T(2,128)} %param.8) | copy-start | bytes 1540
  125.7 162.2 %all-to-all-start.1 = ((bf16[8,8,2048]{2,1,0:T(8,128)(2,1)}), bf16[8,8,2048]{2,1,0:T(8,128)(2,1)S(1)}, u32[]{:S(2)}, u32[]{:S(2)}) async-start(bf16[8,8,2048]{2,1,0:T(8,128)(2,1)} %stack.7), calls=%async_computation.2 | async-start | bytes 524288 | tf_op jit(solution)/shard_map/all_to_all | solution.py:16
  288.6 132.4 %all-to-all-start = ((bf16[8,8,2048]{2,1,0:T(8,128)(2,1)}), bf16[8,8,2048]{2,1,0:T(8,128)(2,1)S(1)}, u32[]{:S(2)}, u32[]{:S(2)}) async-start(bf16[8,8,2048]{2,1,0:T(8,128)(2,1)} %stack.6), calls=%async_computation | async-start | bytes 524288 | tf_op jit(solution)/shard_map/all_to_all | solution.py:16
  294.4 198.6 %reduce-scatter.6.cloned.1.call-start = ((), (), s32[]{:S(2)}) async-start(), calls=%async_computation.9 | async-start | bytes 294912 | tf_op jit(solution)/shard_map/reduce_scatter | solution.py:21
  421.0 22.6 %all-to-all-start.4 = ((bf16[32,4,2048]{2,1,0:T(4,128)(2,1)}), bf16[32,4,2048]{2,1,0:T(4,128)(2,1)S(1)}, u32[]{:S(2)}, u32[]{:S(2)}) async-start(bf16[32,4,2048]{2,1,0:T(4,128)(2,1)} %reshape.134), calls=%async_computation.7 | async-start | bytes 1048576 | tf_op jit(solution)/shard_map/all_to_all | solution.py:71
  425.2 146.0 %reduce-scatter.4.cloned.1.call-start = ((), (), s32[]{:S(2)}) async-start(), calls=%async_computation.8 | async-start | bytes 294912 | tf_op jit(solution)/shard_map/reduce_scatter | solution.py:21
  428.0 5.5 copy-start.7
Sparse Core Ops, SparseCore 0:
  110.6 175.1 reduce-scatter.7
  421.1 71.8 reduce-scatter.5
  497.3 73.8 reduce-scatter.3
Sparse Core Ops, SparseCore 1:
  124.3 288.5 all-reduce.2
